TPU v7x, 256 devices: a whole 4x4x8 slice. The times are simulated.
256 devices in a mesh: leaf: 32 (over y, z), sub: 8 (over x, core).
Axes of the slice: x: 4, y: 4, z: 8, core: 2. Of those that a mesh axis runs over, the one named last changes fastest.
Arguments:
- rhs: float32 [8, 32, 1024, 128], P('sub', 'leaf'), may hold values from -6 to 6
- leaf_block: bfloat16 [8, 32, 1024, 1024], P('sub', 'leaf')
- leaf_inverse: bfloat16 [8, 32, 1024, 1024], P('sub', 'leaf')
- level_basis: float32 [8, 32, 5, 1024, 128], P('sub', 'leaf'), may hold values from -0.1875 to 0.1875
- level_core: float32 [8, 32, 5, 128, 128], P('sub', 'leaf')
- skeleton_basis: float32 [8, 32, 1024, 128], P('sub', 'leaf'), may hold values from -0.1875 to 0.1875
- coupling: float32 [8, 8, 128, 128], P('sub'), may hold values from -0.09375 to 0.09375
Outputs:
- solution: float32 [8, 32, 1024, 128], P('sub', 'leaf')
All inputs are finite; a program needn't handle non-finite values.
Results may differ from a plain program's by a relative error of at most 0.0003.
Values sent between devices are 32-bit elements; how exact they have to be, the bound alone decides.
A program may use at most 64 MiB of HBM per device.

v0:
```python
import jax
import jax.numpy as jnp
from jax import lax
from jax.sharding import PartitionSpec as P

ROUNDS = 2
HI = lax.Precision.HIGHEST


def partner(x, axis, stride):
    return lax.ppermute(x, axis, [(i, i ^ 1 << stride) for i in range(lax.axis_size(axis))])


def matmul(left, right):
    return jnp.dot(left, right, precision=HI, preferred_element_type=jnp.float32)


def tmatmul(left, right):
    return lax.dot_general(
        left, right, (((0,), (0,)), ((), ())), precision=HI, preferred_element_type=jnp.float32
    )


def group_sum(proj, level):
    total = proj
    for bit_num in range(level + 1):
        total = total + partner(total, "leaf", bit_num)
    return total


def inner_solve(field, inverse, basis, core):
    x = matmul(inverse, field)
    depth = lax.axis_size("leaf").bit_length() - 1
    for level in range(depth):
        proj = tmatmul(basis[level], x)
        group = group_sum(proj, level)
        x = x - matmul(basis[level], matmul(core[level], group))
    return x


def body(rhs, leaf_block, leaf_inverse, level_basis, level_core, skeleton_basis, coupling):
    target = rhs[0, 0]
    block = leaf_block[0, 0].astype(jnp.float32)
    inverse = leaf_inverse[0, 0].astype(jnp.float32)
    basis = level_basis[0, 0]
    core = level_core[0, 0]
    skeleton = skeleton_basis[0, 0]
    row_coupling = coupling[0]
    solution = inner_solve(target, inverse, basis, core)
    for outer in range(ROUNDS):
        local_skel = tmatmul(skeleton, solution)
        subtree_total = lax.psum(local_skel, "leaf")
        every_skel = lax.all_gather(subtree_total[None], "sub", axis=0, tiled=True)
        mixed = jnp.einsum(
            "tkj,tjr->kr",
            row_coupling,
            every_skel,
            precision=HI,
            preferred_element_type=jnp.float32,
        )
        applied = matmul(block, solution) + matmul(skeleton, mixed)
        solution = solution + inner_solve(target - applied, inverse, basis, core)
    return solution[None, None]


def solution(mesh):
    return jax.shard_map(
        body,
        mesh=mesh,
        in_specs=(
            P("sub", "leaf", None, None),
            P("sub", "leaf", None, None),
            P("sub", "leaf", None, None),
            P("sub", "leaf", None, None, None),
            P("sub", "leaf", None, None, None),
            P("sub", "leaf", None, None),
            P("sub", None, None, None),
        ),
        out_specs=P("sub", "leaf", None, None),
        check_vma=False,
    )
```

profile of v0, /device:TPU:8, one launch (start us, length us, event | category | flops | bytes accessed | tf_op | source)
XLA Modules:
  0.0 641.4 jit_solution(17399125690273079579)
XLA Ops:
  8.1 3.0 fusion.8
  22.8 3.4 collective-permute-start.2
  32.3 3.0 collective-permute-done.3
  40.6 7.6 %collective-permute-start.5 = (f32[128,128]{0,1:T(8,128)S(1)}, f32[128,128]{0,1:T(8,128)S(1)}, u32[]{:S(2)}, u32[]{:S(2)}) collective-permute-start(f32[128,128]{0,1:T(8,128)S(1)} %add.161), channel_id=1, source_target_pairs={{0,32},{8,40},{16,48},{24,56},{32,0},{40,8},{48,16},{56,24},{64,96... | collective-permute-start | bytes 196616 | tf_op jit(solution)/shard_map/ppermute | solution.py:11
  53.2 3.7 collective-permute-done.6
  58.4 5.2 collective-permute-done.7
  63.6 5.3 collective-permute-start.8
  72.6 3.6 collective-permute-done.9
  78.2 5.1 collective-permute-done.10
  84.4 4.1 collective-permute-done.11
  88.5 4.7 collective-permute-start.12
  93.3 3.5 collective-permute-done.12
  97.6 3.6 collective-permute-done.13
  103.7 3.3 collective-permute-done.14
  109.6 139.8 %all-reduce.3.cloned.1.call-done = f32[1,128,128]{1,2,0:T(8,128)} async-done(((f32[1,128,128]{1,2,0:T(8,128)}), f32[1,128,128]{1,2,0:T(8,128)}) %all-reduce.3.cloned.1.call-update) | async-done | bytes 65552 | tf_op jit(solution)/shard_map/psum | solution.py:52
  250.4 14.0 %all_gather.6 = f32[8,128,128]{2,1,0:T(8,128)S(1)} all-gather(f32[1,128,128]{2,1,0:T(8,128)S(1)} %copy.30), channel_id=1, replica_groups=mesh['leaf'=32,'sub'=8] {'sub'}, dimensions={0}, use_global_device_ids=true | all-gather | bytes 589824 | tf_op jit(solution)/shard_map/all_gather | solution.py:53
  284.6 3.0 collective-permute-done.16
  289.1 3.7 collective-permute-done.17
  296.2 3.0 collective-permute-done.18
  301.3 3.2 collective-permute-done.19
  304.5 4.2 collective-permute-start.20
  308.7 4.1 collective-permute-done.20
  319.4 3.3 collective-permute-start.22
  322.7 2.9 collective-permute-done.22
  325.6 4.1 collective-permute-start.23
  329.7 5.1 collective-permute-done.23
  335.0 4.3 collective-permute-done.24
  341.8 3.7 collective-permute-done.25
  348.0 3.5 collective-permute-done.26
  354.2 6.2 collective-permute-done.27
  360.8 3.9 collective-permute-done.28
  365.7 4.9 collective-permute-done.29
  374.0 136.5 %all-reduce.5.cloned.1.call-done = f32[1,128,128]{1,2,0:T(8,128)} async-done(((f32[1,128,128]{1,2,0:T(8,128)}), f32[1,128,128]{1,2,0:T(8,128)}) %all-reduce.5.cloned.1.call-update) | async-done | bytes 65552 | tf_op jit(solution)/shard_map/psum | solution.py:52
  511.5 13.8 %all_gather.7 = f32[8,128,128]{2,1,0:T(8,128)S(1)} all-gather(f32[1,128,128]{2,1,0:T(8,128)S(1)} %copy.37), channel_id=1, replica_groups=mesh['leaf'=32,'sub'=8] {'sub'}, dimensions={0}, use_global_device_ids=true | all-gather | bytes 589824 | tf_op jit(solution)/shard_map/all_gather | solution.py:53
  545.7 3.0 collective-permute-done.31
  550.3 3.7 collective-permute-done.32
  557.5 3.7 collective-permute-done.33
  562.7 5.2 collective-permute-done.34
  569.8 6.8 %collective-permute-done.35 = f32[128,128]{0,1:T(8,128)S(1)} collective-permute-done((f32[128,128]{0,1:T(8,128)S(1)}, f32[128,128]{0,1:T(8,128)S(1)}, u32[]{:S(2)}, u32[]{:S(2)}) %collective-permute-start.35) | collective-permute-done | bytes 65568 | tf_op jit(solution)/shard_map/ppermute | solution.py:11
  578.6 4.3 collective-permute-done.36
  583.7 4.7 collective-permute-done.37
  590.9 6.5 %collective-permute-done.38 = f32[128,128]{0,1:T(8,128)S(1)} collective-permute-done((f32[128,128]{0,1:T(8,128)S(1)}, f32[128,128]{0,1:T(8,128)S(1)}, u32[]{:S(2)}, u32[]{:S(2)}) %collective-permute-start.38) | collective-permute-done | bytes 65568 | tf_op jit(solution)/shard_map/ppermute | solution.py:11
  598.0 3.7 collective-permute-done.39
  603.8 4.3 collective-permute-done.40
  608.5 5.4 collective-permute-done.41
  615.7 6.5 %collective-permute-done.42 = f32[128,128]{0,1:T(8,128)S(1)} collective-permute-done((f32[128,128]{0,1:T(8,128)S(1)}, f32[128,128]{0,1:T(8,128)S(1)}, u32[]{:S(2)}, u32[]{:S(2)}) %collective-permute-start.42) | collective-permute-done | bytes 65568 | tf_op jit(solution)/shard_map/ppermute | solution.py:11
  622.9 3.7 collective-permute-done.43
  628.0 4.5 collective-permute-done.44
  (164 shorter events, 134.6 us)
Async XLA Ops:
  6.5 242.9 %all-reduce.3.cloned.1.call-start = ((), (), s32[]{:S(2)}) async-start(), calls=%async_computation | async-start | bytes 131072 | tf_op jit(solution)/shard_map/psum | solution.py:52
  12.1 4.4 collective-permute-start
  18.4 4.4 collective-permute-start.1
  22.8 5.6 collective-permute-start.2
  30.3 5.1 collective-permute-start.3
  35.3 5.3 collective-permute-start.4
  40.6 9.8 %collective-permute-start.5 = (f32[128,128]{0,1:T(8,128)S(1)}, f32[128,128]{0,1:T(8,128)S(1)}, u32[]{:S(2)}, u32[]{:S(2)}) collective-permute-start(f32[128,128]{0,1:T(8,128)S(1)} %add.161), channel_id=1, source_target_pairs={{0,32},{8,40},{16,48},{24,56},{32,0},{40,8},{48,16},{56,24},{64,96... | collective-permute-start | bytes 196616 | tf_op jit(solution)/shard_map/ppermute | solution.py:11
  52.3 4.6 collective-permute-start.6
  56.9 6.6 %collective-permute-start.7 = (f32[128,128]{0,1:T(8,128)S(1)}, f32[128,128]{0,1:T(8,128)S(1)}, u32[]{:S(2)}, u32[]{:S(2)}) collective-permute-start(f32[128,128]{0,1:T(8,128)S(1)} %add.163), channel_id=1, source_target_pairs={{0,16},{8,24},{16,0},{24,8},{32,48},{40,56},{48,32},{56,40},{64,80... | collective-permute-start | bytes 196616 | tf_op jit(solution)/shard_map/ppermute | solution.py:11
  63.6 8.3 %collective-permute-start.8 = (f32[128,128]{0,1:T(8,128)S(1)}, f32[128,128]{0,1:T(8,128)S(1)}, u32[]{:S(2)}, u32[]{:S(2)}) collective-permute-start(f32[128,128]{0,1:T(8,128)S(1)} %add.164), channel_id=1, source_target_pairs={{0,32},{8,40},{16,48},{24,56},{32,0},{40,8},{48,16},{56,24},{64,96... | collective-permute-start | bytes 196616 | tf_op jit(solution)/shard_map/ppermute | solution.py:11
  71.8 4.4 collective-permute-start.9
  78.1 5.2 collective-permute-start.10
  83.3 5.3 collective-permute-start.11
  88.5 8.3 %collective-permute-start.12 = (f32[128,128]{0,1:T(8,128)S(1)}, f32[128,128]{0,1:T(8,128)S(1)}, u32[]{:S(2)}, u32[]{:S(2)}) collective-permute-start(f32[128,128]{0,1:T(8,128)S(1)} %add.168), channel_id=1, source_target_pairs={{0,32},{8,40},{16,48},{24,56},{32,0},{40,8},{48,16},{56,24},{64,96... | collective-permute-start | bytes 196616 | tf_op jit(solution)/shard_map/ppermute | solution.py:11
  96.8 4.4 collective-permute-start.13
  101.2 5.9 collective-permute-start.14
  109.6 401.0 %all-reduce.5.cloned.1.call-start = ((), (), s32[]{:S(2)}) async-start(), calls=%async_computation.1 | async-start | bytes 131072 | tf_op jit(solution)/shard_map/psum | solution.py:52
  273.7 4.5 collective-permute-start.15
  283.2 4.4 collective-permute-start.16
  287.6 5.3 collective-permute-start.17
  294.7 4.5 collective-permute-start.18
  299.2 5.3 collective-permute-start.19
  304.5 8.3 %collective-permute-start.20 = (f32[128,128]{0,1:T(8,128)S(1)}, f32[128,128]{0,1:T(8,128)S(1)}, u32[]{:S(2)}, u32[]{:S(2)}) collective-permute-start(f32[128,128]{0,1:T(8,128)S(1)} %add.178), channel_id=1, source_target_pairs={{0,32},{8,40},{16,48},{24,56},{32,0},{40,8},{48,16},{56,24},{64,96... | collective-permute-start | bytes 196616 | tf_op jit(solution)/shard_map/ppermute | solution.py:11
  314.7 4.7 collective-permute-start.21
  319.4 6.2 collective-permute-start.22
  325.6 9.2 %collective-permute-start.23 = (f32[128,128]{0,1:T(8,128)S(1)}, f32[128,128]{0,1:T(8,128)S(1)}, u32[]{:S(2)}, u32[]{:S(2)}) collective-permute-start(f32[128,128]{0,1:T(8,128)S(1)} %add.181), channel_id=1, source_target_pairs={{0,32},{8,40},{16,48},{24,56},{32,0},{40,8},{48,16},{56,24},{64,96... | collective-permute-start | bytes 196616 | tf_op jit(solution)/shard_map/ppermute | solution.py:11
  334.9 4.4 collective-permute-start.24
  341.1 4.4 collective-permute-start.25
  345.5 6.0 collective-permute-start.26
  351.5 9.0 %collective-permute-start.27 = (f32[128,128]{0,1:T(8,128)S(1)}, f32[128,128]{0,1:T(8,128)S(1)}, u32[]{:S(2)}, u32[]{:S(2)}) collective-permute-start(f32[128,128]{0,1:T(8,128)S(1)} %add.185), channel_id=1, source_target_pairs={{0,32},{8,40},{16,48},{24,56},{32,0},{40,8},{48,16},{56,24},{64,96... | collective-permute-start | bytes 196616 | tf_op jit(solution)/shard_map/ppermute | solution.py:11
  360.4 4.4 collective-permute-start.28
  364.8 5.9 collective-permute-start.29
  374.0 153.9 %copy-start.8 = (f32[1024,128]{1,0:T(8,128)S(1)}, f32[1024,128]{1,0:T(8,128)}, u32[]{:S(2)}) copy-start(f32[1024,128]{1,0:T(8,128)} %copy-done.7) | copy-start | bytes 1572868
  534.9 4.5 collective-permute-start.30
  544.4 4.4 collective-permute-start.31
  548.7 5.3 collective-permute-start.32
  555.9 5.3 collective-permute-start.33
  561.2 6.7 %collective-permute-start.34 = (f32[128,128]{0,1:T(8,128)S(1)}, f32[128,128]{0,1:T(8,128)S(1)}, u32[]{:S(2)}, u32[]{:S(2)}) collective-permute-start(f32[128,128]{0,1:T(8,128)S(1)} %add.195), channel_id=1, source_target_pairs={{0,16},{8,24},{16,0},{24,8},{32,48},{40,56},{48,32},{56,40},{64,80... | collective-permute-start | bytes 196616 | tf_op jit(solution)/shard_map/ppermute | solution.py:11
  567.9 8.7 %collective-permute-start.35 = (f32[128,128]{0,1:T(8,128)S(1)}, f32[128,128]{0,1:T(8,128)S(1)}, u32[]{:S(2)}, u32[]{:S(2)}) collective-permute-start(f32[128,128]{0,1:T(8,128)S(1)} %add.196), channel_id=1, source_target_pairs={{0,32},{8,40},{16,48},{24,56},{32,0},{40,8},{48,16},{56,24},{64,96... | collective-permute-start | bytes 196616 | tf_op jit(solution)/shard_map/ppermute | solution.py:11
  578.5 4.4 collective-permute-start.36
  582.9 5.6 collective-permute-start.37
  588.5 8.9 %collective-permute-start.38 = (f32[128,128]{0,1:T(8,128)S(1)}, f32[128,128]{0,1:T(8,128)S(1)}, u32[]{:S(2)}, u32[]{:S(2)}) collective-permute-start(f32[128,128]{0,1:T(8,128)S(1)} %add.199), channel_id=1, source_target_pairs={{0,32},{8,40},{16,48},{24,56},{32,0},{40,8},{48,16},{56,24},{64,96... | collective-permute-start | bytes 196616 | tf_op jit(solution)/shard_map/ppermute | solution.py:11
  597.4 4.4 collective-permute-start.39
  603.7 4.4 collective-permute-start.40
  608.0 6.0 collective-permute-start.41
  614.0 8.3 %collective-permute-start.42 = (f32[128,128]{0,1:T(8,128)S(1)}, f32[128,128]{0,1:T(8,128)S(1)}, u32[]{:S(2)}, u32[]{:S(2)}) collective-permute-start(f32[128,128]{0,1:T(8,128)S(1)} %add.203), channel_id=1, source_target_pairs={{0,32},{8,40},{16,48},{24,56},{32,0},{40,8},{48,16},{56,24},{64,96... | collective-permute-start | bytes 196616 | tf_op jit(solution)/shard_map/ppermute | solution.py:11
  622.3 4.4 collective-permute-start.43
  626.6 5.9 collective-permute-start.44
  (11 other events, 130.3 us)
Sparse Core Ops, SparseCore 0:
  109.7 139.6 all-reduce.2
  374.1 136.3 all-reduce.4
where the time goes:
time: 651 us; the launch traced here: 641 us
  waiting for transfers between devices  450 us (69%)
  starting transfers between devices  83.4 us (13%)
  matrix products  57.5 us (9%)
  blocking collectives  27.7 us (4%)
  between operations  14.4 us (2%)
  local copies, waits for them, and re-layouts  8.09 us (1%)
    psum x2, waiting for transfers between devices, body(): subtree_total = lax.psum(local_skel, 'leaf')  276 us
    ppermute x45, waiting for transfers between devices, partner(): lax.ppermute(x, axis, [(i, i ^ 1 << stride) for i in range(lax.axis_size(...  174 us
    ppermute x45, starting transfers between devices, partner(): lax.ppermute(x, axis, [(i, i ^ 1 << stride) for i in range(lax.axis_size(...  83.4 us
    dot_general x37, matrix products, matmul(): jnp.dot(left, right, precision=HI, preferred_element_type=jnp.float32)  31.4 us
    all_gather x2, blocking collectives, body(): every_skel = lax.all_gather(subtree_total[None], 'sub', axis=0, tiled=True)  27.7 us
    dot_general x17, matrix products, tmatmul(): lax.dot_general(left, right, (((0,), (0,)), ((), ())), precision=HI, pref...  22 us
  transfers between devices with their start and end apart: 47, of which 47 were waited for; matrix products, arithmetic and copies ran while one was open for 0% of the time, Pallas kernels for 0%

commit v1 on v0

--- a/solution.py
+++ b/solution.py
@@ -2,6 +2,7 @@
 import jax.numpy as jnp
 from jax import lax
 from jax.sharding import PartitionSpec as P
+from jax.lax import all_gather
 
 ROUNDS = 2
 HI = lax.Precision.HIGHEST
@@ -49,7 +50,7 @@
     solution = inner_solve(target, inverse, basis, core)
     for outer in range(ROUNDS):
         local_skel = tmatmul(skeleton, solution)
-        subtree_total = lax.psum(local_skel, "leaf")
+        subtree_total = all_gather(local_skel, axis_name="leaf").sum(axis=0)
         every_skel = lax.all_gather(subtree_total[None], "sub", axis=0, tiled=True)
         mixed = jnp.einsum(
             "tkj,tjr->kr",

time: 651 us -> 521 us (0.80)
  waiting for transfers between devices: 450 us -> 303 us
  starting transfers between devices: 83.4 us -> 102 us
    psum x2 -> x0, waiting for transfers between devices: 276 us -> none  [body(): subtree_total = lax.psum(local_skel, 'leaf')]
    all_gather x0 -> x2, waiting for transfers between devices: none -> 149 us  [body(): subtree_total = all_gather(local_skel, axis_name='leaf').sum(axis=0)]
    ppermute x45, waiting for transfers between devices: 174 us -> 154 us  [partner(): lax.ppermute(x, axis, [(i, i ^ 1 << stride) for i in range(lax.axis_size(...]
    ppermute x45, starting transfers between devices: 83.4 us -> 102 us  [partner(): lax.ppermute(x, axis, [(i, i ^ 1 << stride) for i in range(lax.axis_size(...]
  transfers between devices with their start and end apart: 47 -> 47, of which waited for: 47 -> 47; matrix products, arithmetic and copies ran while one was open for 0% -> 1% of each run, Pallas kernels for 0% -> 0%
where the time goes in v1:
time: 521 us; the launch traced here: 512 us
  waiting for transfers between devices  303 us (58%)
  starting transfers between devices  102 us (20%)
  matrix products  53.5 us (10%)
  blocking collectives  27.7 us (5%)
  between operations  14.4 us (3%)
  local copies, waits for them, and re-layouts  10.3 us (2%)
    ppermute x45, waiting for transfers between devices, partner(): lax.ppermute(x, axis, [(i, i ^ 1 << stride) for i in range(lax.axis_size(...  154 us
    all_gather x2, waiting for transfers between devices, body(): subtree_total = all_gather(local_skel, axis_name='leaf').sum(axis=0)  149 us
    ppermute x45, starting transfers between devices, partner(): lax.ppermute(x, axis, [(i, i ^ 1 << stride) for i in range(lax.axis_size(...  102 us
    dot_general x37, matrix products, matmul(): jnp.dot(left, right, precision=HI, preferred_element_type=jnp.float32)  30.3 us
    all_gather x2, blocking collectives, body(): every_skel = lax.all_gather(subtree_total[None], 'sub', axis=0, tiled=True)  27.7 us
    dot_general x17, matrix products, tmatmul(): lax.dot_general(left, right, (((0,), (0,)), ((), ())), precision=HI, pref...  22 us
  transfers between devices with their start and end apart: 47, of which 47 were waited for; matrix products, arithmetic and copies ran while one was open for 1% of the time, Pallas kernels for 0%

profile of v1, /device:TPU:8, one launch (start us, length us, event | category | flops | bytes accessed | tf_op | source)
XLA Modules:
  0.0 511.7 jit_solution(12410502471732345382)
XLA Ops:
  8.1 3.0 fusion.8
  22.8 3.4 collective-permute-start.2
  32.3 3.0 collective-permute-done.3
  40.6 7.6 %collective-permute-start.5 = (f32[128,128]{0,1:T(8,128)S(1)}, f32[128,128]{0,1:T(8,128)S(1)}, u32[]{:S(2)}, u32[]{:S(2)}) collective-permute-start(f32[128,128]{0,1:T(8,128)S(1)} %add.157), channel_id=1, source_target_pairs={{0,32},{8,40},{16,48},{24,56},{32,0},{40,8},{48,16},{56,24},{64,96... | collective-permute-start | bytes 196616 | tf_op jit(solution)/shard_map/ppermute | solution.py:12
  53.2 3.7 collective-permute-done.6
  58.4 5.2 %collective-permute-done.7 = f32[128,128]{0,1:T(8,128)S(1)} collective-permute-done((f32[128,128]{0,1:T(8,128)S(1)}, f32[128,128]{0,1:T(8,128)S(1)}, u32[]{:S(2)}, u32[]{:S(2)}) %collective-permute-start.7) | collective-permute-done | bytes 65568 | tf_op jit(solution)/shard_map/ppermute | solution.py:12
  63.6 5.3 %collective-permute-start.8 = (f32[128,128]{0,1:T(8,128)S(1)}, f32[128,128]{0,1:T(8,128)S(1)}, u32[]{:S(2)}, u32[]{:S(2)}) collective-permute-start(f32[128,128]{0,1:T(8,128)S(1)} %add.160), channel_id=1, source_target_pairs={{0,32},{8,40},{16,48},{24,56},{32,0},{40,8},{48,16},{56,24},{64,96... | collective-permute-start | bytes 196616 | tf_op jit(solution)/shard_map/ppermute | solution.py:12
  68.9 2.9 collective-permute-done.8
  72.6 3.6 collective-permute-done.9
  78.2 5.1 collective-permute-done.10
  84.4 4.1 collective-permute-done.11
  88.5 4.7 collective-permute-start.12
  93.3 3.5 collective-permute-done.12
  97.6 3.6 collective-permute-done.13
  103.7 3.3 collective-permute-done.14
  109.6 75.6 %all-gather.7.cloned.1.call-done = f32[4096,128]{0,1:T(8,128)} async-done(((f32[128,128]{0,1:T(8,128)}), f32[4096,128]{0,1:T(8,128)}) %all-gather.7.cloned.1.call-update) | async-done | bytes 2097168 | tf_op jit(solution)/shard_map/all_gather | solution.py:53
  187.5 14.0 %all-gather.1 = f32[1024,128]{0,1:T(8,128)S(1)} all-gather(f32[128,128]{0,1:T(8,128)S(1)} %bitcast_reduce_fusion.1), channel_id=3, replica_groups=mesh['leaf'=32,'sub'=8] {'sub'}, dimensions={0}, use_global_device_ids=true | all-gather | bytes 589824 | tf_op jit(solution)/shard_map/all_gather | solution.py:54
  220.3 2.9 collective-permute-done.16
  225.4 3.1 collective-permute-done.17
  234.7 3.1 collective-permute-start.19
  240.2 3.6 collective-permute-start.20
  243.8 4.7 collective-permute-done.20
  255.1 4.6 collective-permute-start.22
  259.7 2.9 collective-permute-done.22
  265.1 5.9 %collective-permute-done.23 = f32[128,128]{0,1:T(8,128)S(1)} collective-permute-done((f32[128,128]{0,1:T(8,128)S(1)}, f32[128,128]{0,1:T(8,128)S(1)}, u32[]{:S(2)}, u32[]{:S(2)}) %collective-permute-start.23) | collective-permute-done | bytes 65568 | tf_op jit(solution)/shard_map/ppermute | solution.py:12
  271.1 4.2 collective-permute-done.24
  278.6 3.6 collective-permute-done.25
  284.5 3.7 collective-permute-done.26
  290.3 6.2 %collective-permute-done.27 = f32[128,128]{0,1:T(8,128)S(1)} collective-permute-done((f32[128,128]{0,1:T(8,128)S(1)}, f32[128,128]{0,1:T(8,128)S(1)}, u32[]{:S(2)}, u32[]{:S(2)}) %collective-permute-start.27) | collective-permute-done | bytes 65568 | tf_op jit(solution)/shard_map/ppermute | solution.py:12
  296.6 4.3 collective-permute-done.28
  303.5 3.3 collective-permute-done.29
  310.1 73.5 %all-gather.9.cloned.1.call-done = f32[4096,128]{0,1:T(8,128)} async-done(((f32[128,128]{0,1:T(8,128)}), f32[4096,128]{0,1:T(8,128)}) %all-gather.9.cloned.1.call-update) | async-done | bytes 2097168 | tf_op jit(solution)/shard_map/all_gather | solution.py:53
  386.0 13.8 %all-gather.3 = f32[1024,128]{0,1:T(8,128)S(1)} all-gather(f32[128,128]{0,1:T(8,128)S(1)} %bitcast_reduce_fusion), channel_id=5, replica_groups=mesh['leaf'=32,'sub'=8] {'sub'}, dimensions={0}, use_global_device_ids=true | all-gather | bytes 589824 | tf_op jit(solution)/shard_map/all_gather | solution.py:54
  422.9 3.1 collective-permute-done.32
  429.3 2.9 collective-permute-done.33
  432.2 3.2 collective-permute-start.34
  438.0 3.4 collective-permute-start.35
  441.4 4.8 collective-permute-done.35
  452.7 4.3 collective-permute-start.37
  457.0 2.9 collective-permute-done.37
  462.8 5.5 %collective-permute-done.38 = f32[128,128]{0,1:T(8,128)S(1)} collective-permute-done((f32[128,128]{0,1:T(8,128)S(1)}, f32[128,128]{0,1:T(8,128)S(1)}, u32[]{:S(2)}, u32[]{:S(2)}) %collective-permute-start.38) | collective-permute-done | bytes 65568 | tf_op jit(solution)/shard_map/ppermute | solution.py:12
  468.7 3.9 collective-permute-done.39
  475.9 3.0 collective-permute-done.40
  479.0 3.0 collective-permute-start.41
  484.3 3.6 collective-permute-start.42
  487.9 4.7 collective-permute-done.42
  493.0 3.9 collective-permute-done.43
  499.0 3.7 collective-permute-done.44
  (172 shorter events, 146.3 us)
Async XLA Ops:
  6.5 178.7 %all-gather.7.cloned.1.call-start = ((), (), s32[]{:S(2)}) async-start(), calls=%async_computation | async-start | bytes 2162688 | tf_op jit(solution)/shard_map/all_gather | solution.py:53
  12.1 4.4 collective-permute-start
  18.4 4.4 collective-permute-start.1
  22.8 5.6 %collective-permute-start.2 = (f32[128,128]{0,1:T(8,128)S(1)}, f32[128,128]{0,1:T(8,128)S(1)}, u32[]{:S(2)}, u32[]{:S(2)}) collective-permute-start(f32[128,128]{0,1:T(8,128)S(1)} %add.154), channel_id=1, source_target_pairs={{0,16},{8,24},{16,0},{24,8},{32,48},{40,56},{48,32},{56,40},{64,80... | collective-permute-start | bytes 196616 | tf_op jit(solution)/shard_map/ppermute | solution.py:12
  30.3 5.1 collective-permute-start.3
  35.3 5.3 %collective-permute-start.4 = (f32[128,128]{0,1:T(8,128)S(1)}, f32[128,128]{0,1:T(8,128)S(1)}, u32[]{:S(2)}, u32[]{:S(2)}) collective-permute-start(f32[128,128]{0,1:T(8,128)S(1)} %add.156), channel_id=1, source_target_pairs={{0,16},{8,24},{16,0},{24,8},{32,48},{40,56},{48,32},{56,40},{64,80... | collective-permute-start | bytes 196616 | tf_op jit(solution)/shard_map/ppermute | solution.py:12
  40.6 9.8 %collective-permute-start.5 = (f32[128,128]{0,1:T(8,128)S(1)}, f32[128,128]{0,1:T(8,128)S(1)}, u32[]{:S(2)}, u32[]{:S(2)}) collective-permute-start(f32[128,128]{0,1:T(8,128)S(1)} %add.157), channel_id=1, source_target_pairs={{0,32},{8,40},{16,48},{24,56},{32,0},{40,8},{48,16},{56,24},{64,96... | collective-permute-start | bytes 196616 | tf_op jit(solution)/shard_map/ppermute | solution.py:12
  52.3 4.6 collective-permute-start.6
  56.9 6.6 %collective-permute-start.7 = (f32[128,128]{0,1:T(8,128)S(1)}, f32[128,128]{0,1:T(8,128)S(1)}, u32[]{:S(2)}, u32[]{:S(2)}) collective-permute-start(f32[128,128]{0,1:T(8,128)S(1)} %add.159), channel_id=1, source_target_pairs={{0,16},{8,24},{16,0},{24,8},{32,48},{40,56},{48,32},{56,40},{64,80... | collective-permute-start | bytes 196616 | tf_op jit(solution)/shard_map/ppermute | solution.py:12
  63.6 8.3 %collective-permute-start.8 = (f32[128,128]{0,1:T(8,128)S(1)}, f32[128,128]{0,1:T(8,128)S(1)}, u32[]{:S(2)}, u32[]{:S(2)}) collective-permute-start(f32[128,128]{0,1:T(8,128)S(1)} %add.160), channel_id=1, source_target_pairs={{0,32},{8,40},{16,48},{24,56},{32,0},{40,8},{48,16},{56,24},{64,96... | collective-permute-start | bytes 196616 | tf_op jit(solution)/shard_map/ppermute | solution.py:12
  71.8 4.4 collective-permute-start.9
  76.5 31.5 %copy-start.6 = (f32[1,1,1024,128]{3,2,1,0:T(8,128)S(1)}, f32[1,1,1024,128]{3,2,1,0:T(8,128)}, u32[]{:S(2)}) copy-start(f32[1,1,1024,128]{3,2,1,0:T(8,128)} %param.12) | copy-start | bytes 1572868
  78.1 5.2 %collective-permute-start.10 = (f32[128,128]{0,1:T(8,128)S(1)}, f32[128,128]{0,1:T(8,128)S(1)}, u32[]{:S(2)}, u32[]{:S(2)}) collective-permute-start(f32[128,128]{0,1:T(8,128)S(1)} %convolution_bitcast_fusion.19), channel_id=1, source_target_pairs={{0,8},{8,0},{16,24},{24,16},{32,40},{40,32},{48,56},{56,48},{64,72... | collective-permute-start | bytes 196616 | tf_op jit(solution)/shard_map/ppermute | solution.py:12
  83.3 5.3 %collective-permute-start.11 = (f32[128,128]{0,1:T(8,128)S(1)}, f32[128,128]{0,1:T(8,128)S(1)}, u32[]{:S(2)}, u32[]{:S(2)}) collective-permute-start(f32[128,128]{0,1:T(8,128)S(1)} %add.163), channel_id=1, source_target_pairs={{0,16},{8,24},{16,0},{24,8},{32,48},{40,56},{48,32},{56,40},{64,80... | collective-permute-start | bytes 196616 | tf_op jit(solution)/shard_map/ppermute | solution.py:12
  88.5 8.3 %collective-permute-start.12 = (f32[128,128]{0,1:T(8,128)S(1)}, f32[128,128]{0,1:T(8,128)S(1)}, u32[]{:S(2)}, u32[]{:S(2)}) collective-permute-start(f32[128,128]{0,1:T(8,128)S(1)} %add.164), channel_id=1, source_target_pairs={{0,32},{8,40},{16,48},{24,56},{32,0},{40,8},{48,16},{56,24},{64,96... | collective-permute-start | bytes 196616 | tf_op jit(solution)/shard_map/ppermute | solution.py:12
  96.8 4.4 collective-permute-start.13
  101.2 5.9 %collective-permute-start.14 = (f32[128,128]{0,1:T(8,128)S(1)}, f32[128,128]{0,1:T(8,128)S(1)}, u32[]{:S(2)}, u32[]{:S(2)}) collective-permute-start(f32[128,128]{0,1:T(8,128)S(1)} %add.166), channel_id=1, source_target_pairs={{0,128},{8,136},{16,144},{24,152},{32,160},{40,168},{48,176},{56,1... | collective-permute-start | bytes 196616 | tf_op jit(solution)/shard_map/ppermute | solution.py:12
  109.6 274.1 %all-gather.9.cloned.1.call-start = ((), (), s32[]{:S(2)}) async-start(), calls=%async_computation.1 | async-start | bytes 2162688 | tf_op jit(solution)/shard_map/all_gather | solution.py:53
  209.3 4.5 collective-permute-start.15
  218.8 4.4 collective-permute-start.16
  223.2 5.3 %collective-permute-start.17 = (f32[128,128]{0,1:T(8,128)S(1)}, f32[128,128]{0,1:T(8,128)S(1)}, u32[]{:S(2)}, u32[]{:S(2)}) collective-permute-start(f32[128,128]{0,1:T(8,128)S(1)} %add.171), channel_id=1, source_target_pairs={{0,16},{8,24},{16,0},{24,8},{32,48},{40,56},{48,32},{56,40},{64,80... | collective-permute-start | bytes 196616 | tf_op jit(solution)/shard_map/ppermute | solution.py:12
  230.3 4.4 collective-permute-start.18
  234.7 5.5 %collective-permute-start.19 = (f32[128,128]{0,1:T(8,128)S(1)}, f32[128,128]{0,1:T(8,128)S(1)}, u32[]{:S(2)}, u32[]{:S(2)}) collective-permute-start(f32[128,128]{0,1:T(8,128)S(1)} %add.173), channel_id=1, source_target_pairs={{0,16},{8,24},{16,0},{24,8},{32,48},{40,56},{48,32},{56,40},{64,80... | collective-permute-start | bytes 196616 | tf_op jit(solution)/shard_map/ppermute | solution.py:12
  240.2 8.3 %collective-permute-start.20 = (f32[128,128]{0,1:T(8,128)S(1)}, f32[128,128]{0,1:T(8,128)S(1)}, u32[]{:S(2)}, u32[]{:S(2)}) collective-permute-start(f32[128,128]{0,1:T(8,128)S(1)} %add.174), channel_id=1, source_target_pairs={{0,32},{8,40},{16,48},{24,56},{32,0},{40,8},{48,16},{56,24},{64,96... | collective-permute-start | bytes 196616 | tf_op jit(solution)/shard_map/ppermute | solution.py:12
  250.4 4.7 collective-permute-start.21
  255.1 7.5 %collective-permute-start.22 = (f32[128,128]{0,1:T(8,128)S(1)}, f32[128,128]{0,1:T(8,128)S(1)}, u32[]{:S(2)}, u32[]{:S(2)}) collective-permute-start(f32[128,128]{0,1:T(8,128)S(1)} %add.176), channel_id=1, source_target_pairs={{0,16},{8,24},{16,0},{24,8},{32,48},{40,56},{48,32},{56,40},{64,80... | collective-permute-start | bytes 196616 | tf_op jit(solution)/shard_map/ppermute | solution.py:12
  262.6 8.4 %collective-permute-start.23 = (f32[128,128]{0,1:T(8,128)S(1)}, f32[128,128]{0,1:T(8,128)S(1)}, u32[]{:S(2)}, u32[]{:S(2)}) collective-permute-start(f32[128,128]{0,1:T(8,128)S(1)} %add.177), channel_id=1, source_target_pairs={{0,32},{8,40},{16,48},{24,56},{32,0},{40,8},{48,16},{56,24},{64,96... | collective-permute-start | bytes 196616 | tf_op jit(solution)/shard_map/ppermute | solution.py:12
  271.0 4.4 collective-permute-start.24
  277.2 5.0 collective-permute-start.25
  282.3 6.0 %collective-permute-start.26 = (f32[128,128]{0,1:T(8,128)S(1)}, f32[128,128]{0,1:T(8,128)S(1)}, u32[]{:S(2)}, u32[]{:S(2)}) collective-permute-start(f32[128,128]{0,1:T(8,128)S(1)} %add.180), channel_id=1, source_target_pairs={{0,16},{8,24},{16,0},{24,8},{32,48},{40,56},{48,32},{56,40},{64,80... | collective-permute-start | bytes 196616 | tf_op jit(solution)/shard_map/ppermute | solution.py:12
  288.3 8.3 %collective-permute-start.27 = (f32[128,128]{0,1:T(8,128)S(1)}, f32[128,128]{0,1:T(8,128)S(1)}, u32[]{:S(2)}, u32[]{:S(2)}) collective-permute-start(f32[128,128]{0,1:T(8,128)S(1)} %add.181), channel_id=1, source_target_pairs={{0,32},{8,40},{16,48},{24,56},{32,0},{40,8},{48,16},{56,24},{64,96... | collective-permute-start | bytes 196616 | tf_op jit(solution)/shard_map/ppermute | solution.py:12
  296.5 4.4 collective-permute-start.28
  300.9 5.9 %collective-permute-start.29 = (f32[128,128]{0,1:T(8,128)S(1)}, f32[128,128]{0,1:T(8,128)S(1)}, u32[]{:S(2)}, u32[]{:S(2)}) collective-permute-start(f32[128,128]{0,1:T(8,128)S(1)} %add.183), channel_id=1, source_target_pairs={{0,128},{8,136},{16,144},{24,152},{32,160},{40,168},{48,176},{56,1... | collective-permute-start | bytes 196616 | tf_op jit(solution)/shard_map/ppermute | solution.py:12
  406.8 4.5 collective-permute-start.30
  416.3 4.4 collective-permute-start.31
  420.7 5.3 %collective-permute-start.32 = (f32[128,128]{0,1:T(8,128)S(1)}, f32[128,128]{0,1:T(8,128)S(1)}, u32[]{:S(2)}, u32[]{:S(2)}) collective-permute-start(f32[128,128]{0,1:T(8,128)S(1)} %add.189), channel_id=1, source_target_pairs={{0,16},{8,24},{16,0},{24,8},{32,48},{40,56},{48,32},{56,40},{64,80... | collective-permute-start | bytes 196616 | tf_op jit(solution)/shard_map/ppermute | solution.py:12
  427.8 4.4 collective-permute-start.33
  432.2 5.8 %collective-permute-start.34 = (f32[128,128]{0,1:T(8,128)S(1)}, f32[128,128]{0,1:T(8,128)S(1)}, u32[]{:S(2)}, u32[]{:S(2)}) collective-permute-start(f32[128,128]{0,1:T(8,128)S(1)} %add.191), channel_id=1, source_target_pairs={{0,16},{8,24},{16,0},{24,8},{32,48},{40,56},{48,32},{56,40},{64,80... | collective-permute-start | bytes 196616 | tf_op jit(solution)/shard_map/ppermute | solution.py:12
  438.0 8.3 %collective-permute-start.35 = (f32[128,128]{0,1:T(8,128)S(1)}, f32[128,128]{0,1:T(8,128)S(1)}, u32[]{:S(2)}, u32[]{:S(2)}) collective-permute-start(f32[128,128]{0,1:T(8,128)S(1)} %add.192), channel_id=1, source_target_pairs={{0,32},{8,40},{16,48},{24,56},{32,0},{40,8},{48,16},{56,24},{64,96... | collective-permute-start | bytes 196616 | tf_op jit(solution)/shard_map/ppermute | solution.py:12
  448.1 4.6 collective-permute-start.36
  452.7 7.2 %collective-permute-start.37 = (f32[128,128]{0,1:T(8,128)S(1)}, f32[128,128]{0,1:T(8,128)S(1)}, u32[]{:S(2)}, u32[]{:S(2)}) collective-permute-start(f32[128,128]{0,1:T(8,128)S(1)} %add.194), channel_id=1, source_target_pairs={{0,16},{8,24},{16,0},{24,8},{32,48},{40,56},{48,32},{56,40},{64,80... | collective-permute-start | bytes 196616 | tf_op jit(solution)/shard_map/ppermute | solution.py:12
  460.0 8.3 %collective-permute-start.38 = (f32[128,128]{0,1:T(8,128)S(1)}, f32[128,128]{0,1:T(8,128)S(1)}, u32[]{:S(2)}, u32[]{:S(2)}) collective-permute-start(f32[128,128]{0,1:T(8,128)S(1)} %add.195), channel_id=1, source_target_pairs={{0,32},{8,40},{16,48},{24,56},{32,0},{40,8},{48,16},{56,24},{64,96... | collective-permute-start | bytes 196616 | tf_op jit(solution)/shard_map/ppermute | solution.py:12
  468.3 4.4 collective-permute-start.39
  474.5 4.4 collective-permute-start.40
  479.0 5.3 %collective-permute-start.41 = (f32[128,128]{0,1:T(8,128)S(1)}, f32[128,128]{0,1:T(8,128)S(1)}, u32[]{:S(2)}, u32[]{:S(2)}) collective-permute-start(f32[128,128]{0,1:T(8,128)S(1)} %add.198), channel_id=1, source_target_pairs={{0,16},{8,24},{16,0},{24,8},{32,48},{40,56},{48,32},{56,40},{64,80... | collective-permute-start | bytes 196616 | tf_op jit(solution)/shard_map/ppermute | solution.py:12
  484.3 8.3 %collective-permute-start.42 = (f32[128,128]{0,1:T(8,128)S(1)}, f32[128,128]{0,1:T(8,128)S(1)}, u32[]{:S(2)}, u32[]{:S(2)}) collective-permute-start(f32[128,128]{0,1:T(8,128)S(1)} %add.199), channel_id=1, source_target_pairs={{0,32},{8,40},{16,48},{24,56},{32,0},{40,8},{48,16},{56,24},{64,96... | collective-permute-start | bytes 196616 | tf_op jit(solution)/shard_map/ppermute | solution.py:12
  492.5 4.4 collective-permute-start.43
  496.9 5.9 %collective-permute-start.44 = (f32[128,128]{0,1:T(8,128)S(1)}, f32[128,128]{0,1:T(8,128)S(1)}, u32[]{:S(2)}, u32[]{:S(2)}) collective-permute-start(f32[128,128]{0,1:T(8,128)S(1)} %add.201), channel_id=1, source_target_pairs={{0,128},{8,136},{16,144},{24,152},{32,160},{40,168},{48,176},{56,1... | collective-permute-start | bytes 196616 | tf_op jit(solution)/shard_map/ppermute | solution.py:12
  (14 other events, 157.7 us)
Sparse Core Ops, SparseCore 0:
  109.7 75.4 all-gather.6
  310.3 73.3 all-gather.8
